TPU v7x, 512 devices: a whole 4x4x16 slice. The times are simulated.
512 devices in a mesh: seq: 32 (over y_hi, z), head: 16 (over y_lo, x, core).
Axes of the slice: x: 4, y: 4 (y_hi: 2, y_lo: 2; y = y_hi * 2 + y_lo), z: 16, core: 2. Of those that a mesh axis runs over, the one named last changes fastest.
Arguments:
- queries: bfloat16 [8192, 6144], P('seq', 'head'), may hold values from -42 to 42
- keys: bfloat16 [8192, 6144], P('seq', 'head'), may hold values from -4 to 4
- values: bfloat16 [8192, 6144], P('seq', 'head'), may hold values from -120 to 120
- block_mask: int32 [64, 64], P('seq'), may hold values from 0 to 1
- region_of_block: int32 [64], P('seq'), may hold values from 0 to 7
- text_keys: bfloat16 [8, 256, 6144], P(None, 'seq', 'head'), may hold values from -4 to 4
- text_values: bfloat16 [8, 256, 6144], P(None, 'seq', 'head'), may hold values from -6 to 6
- gain: bfloat16 [6144], P('head'), may hold values from 0.099609375 to 1.8984375
Outputs:
- mixed: bfloat16 [8192, 6144], P('seq', 'head')
All inputs are finite; a program needn't handle non-finite values.
Results may differ from a plain program's by a relative error of at most 0.0085.
Values may be sent and summed in bfloat16 or wider, within the bound.
A program may use at most 64 MiB of HBM per device.

v0:
```python
import jax
import jax.numpy as jnp
from jax import lax
from jax.sharding import PartitionSpec as P

HEADS = 48
HD = 128
BLK = 128
TXT = 256


def absorb(carry, query_rows, key_block, value_block, tile, softmax_scale):
    top, total, accum = carry
    keep = jnp.repeat(jnp.repeat(tile, BLK, axis=0), BLK, axis=1)
    scores = (
        jnp.einsum("qhd,khd->hqk", query_rows, key_block, preferred_element_type=jnp.float32)
        * softmax_scale
    )
    scores = jnp.where(keep[None], scores, -1e30)
    new_top = jnp.maximum(top, jnp.max(scores, axis=-1))
    weights = jnp.where(keep[None], jnp.exp(scores - new_top[..., None]), 0.0)
    factor = jnp.exp(top - new_top)
    total = total * factor + jnp.sum(weights, axis=-1)
    update = jnp.einsum(
        "hqk,khd->hqd",
        weights.astype(jnp.bfloat16),
        value_block,
        preferred_element_type=jnp.float32,
    )
    accum = accum * factor[..., None] + update
    return (new_top, total, accum)


def local(queries, keys, values, block_mask, region_of_block, text_keys, text_values, gain):
    tok, width = queries.shape
    heads = width // HD
    blocks = tok // BLK
    softmax_scale = HD ** (-0.5)
    first = lax.axis_index("seq") * blocks
    columns = jnp.arange(block_mask.shape[1], dtype=jnp.int32)
    owned = first + jnp.arange(blocks, dtype=jnp.int32)
    allowed = (block_mask > 0) | (columns[None, :] == owned[:, None])
    query_rows = queries.reshape(tok, heads, HD)
    start_state = (
        jnp.full((heads, tok), -1e30, jnp.float32),
        jnp.zeros((heads, tok), jnp.float32),
        jnp.zeros((heads, tok, HD), jnp.float32),
    )
    key_piece = lax.all_gather(keys, "seq", axis=0, tiled=True)
    value_piece = lax.all_gather(values, "seq", axis=0, tiled=True)
    rows = key_piece.shape[0]
    stride = 2 * tok

    def inner(index, carry):
        offset = index * stride
        key_block = lax.dynamic_slice_in_dim(key_piece, offset, stride, 0).reshape(
            stride, heads, HD
        )
        value_block = lax.dynamic_slice_in_dim(value_piece, offset, stride, 0).reshape(
            stride, heads, HD
        )
        tile = lax.dynamic_slice_in_dim(allowed, offset // BLK, stride // BLK, 1)
        return absorb(carry, query_rows, key_block, value_block, tile, softmax_scale)

    state = lax.fori_loop(0, rows // stride, inner, start_state)
    region_panel_key_rows, region_panel_value_rows = (
        lax.all_gather(text_keys, "seq", axis=1, tiled=True),
        lax.all_gather(text_values, "seq", axis=1, tiled=True),
    )
    top, total, accum = state
    self_out = jnp.transpose(accum / total[..., None], (1, 0, 2)).reshape(tok, width)
    chosen_keys = region_panel_key_rows[region_of_block].reshape(blocks, TXT, heads, HD)
    chosen_values = region_panel_value_rows[region_of_block].reshape(blocks, TXT, heads, HD)
    query_block_groups = queries.reshape(blocks, BLK, heads, HD)
    caption_score_matrix = (
        jnp.einsum(
            "bqhd,bthd->bhqt", query_block_groups, chosen_keys, preferred_element_type=jnp.float32
        )
        * softmax_scale
    )
    text_top = jnp.max(caption_score_matrix, axis=-1, keepdims=True)
    text_weights = jnp.exp(caption_score_matrix - text_top)
    caption_score_sum = jnp.sum(text_weights, axis=-1)
    cross_sum = jnp.einsum(
        "bhqt,bthd->bqhd",
        text_weights.astype(jnp.bfloat16),
        chosen_values,
        preferred_element_type=jnp.float32,
    )
    cross_out = (cross_sum / jnp.transpose(caption_score_sum, (0, 2, 1))[..., None]).reshape(
        tok, width
    )
    combined = self_out + cross_out
    squares = jnp.sum(combined * combined, axis=1)
    square_total = lax.psum(squares, "head")
    mean_square = square_total / (HEADS * HD)
    scaled = combined * lax.rsqrt(mean_square + 1e-06)[:, None] * gain.astype(jnp.float32)[None, :]
    return scaled.astype(jnp.bfloat16)


def solution(mesh):
    in_specs = (
        P("seq", "head"),
        P("seq", "head"),
        P("seq", "head"),
        P("seq", None),
        P("seq"),
        P(None, "seq", "head"),
        P(None, "seq", "head"),
        P("head"),
    )
    out_specs = P("seq", "head")
    return jax.shard_map(local, mesh=mesh, in_specs=in_specs, out_specs=out_specs, check_vma=False)
```

profile of v0, /device:TPU:1, one launch (start us, length us, event | category | flops | bytes accessed | tf_op | source)
XLA Modules:
  0.0 747.4 jit_solution(13527715328726537299)
XLA Ops:
  6.6 0.7 all-gather.11.cloned.1.call-update
  7.3 0.7 all-gather.9.cloned.1.call-update
  8.1 1.7 copy.37
  9.9 1.7 copy.39
  11.6 1.0 reshape.95
  13.2 133.5 %all-gather.11.cloned.1.call-done = bf16[8,256,384]{2,1,0:T(8,128)(2,1)} async-done(((bf16[8,8,384]{2,1,0:T(8,128)(2,1)}), bf16[8,256,384]{2,1,0:T(8,128)(2,1)}) %all-gather.11.cloned.1.call-update) | async-done | bytes 1572880 | tf_op jit(solution)/shard_map/all_gather | solution.py:67
  146.7 2.0 gather_fusion.1
  148.9 135.7 %all-gather.9.cloned.1.call-done = bf16[8,256,384]{2,1,0:T(8,128)(2,1)} async-done(((bf16[8,8,384]{2,1,0:T(8,128)(2,1)}), bf16[8,256,384]{2,1,0:T(8,128)(2,1)}) %all-gather.9.cloned.1.call-update) | async-done | bytes 1572880 | tf_op jit(solution)/shard_map/all_gather | solution.py:68
  284.6 2.0 gather_fusion
  288.1 183.3 %all-gather.5.cloned.1.call-done = bf16[8192,384]{0,1:T(8,128)(2,1)} async-done(((bf16[256,384]{0,1:T(8,128)(2,1)}), bf16[8192,384]{0,1:T(8,128)(2,1)}) %all-gather.5.cloned.1.call-update) | async-done | bytes 6291472 | tf_op jit(solution)/shard_map/all_gather | solution.py:49
  471.4 185.5 %all-gather.7.cloned.1.call-done = bf16[8192,384]{0,1:T(8,128)(2,1)} async-done(((bf16[256,384]{0,1:T(8,128)(2,1)}), bf16[8192,384]{0,1:T(8,128)(2,1)}) %all-gather.7.cloned.1.call-update) | async-done | bytes 6291472 | tf_op jit(solution)/shard_map/all_gather | solution.py:50
  656.8 46.9 %while.20 = (s32[]{:T(128)}, f32[3,256]{1,0:T(4,128)S(1)}, f32[3,256]{1,0:T(4,128)S(1)}, f32[3,256,128]{2,1,0:T(8,128)S(1)}, pred[2,64]{1,0:T(4,128)(4,1)S(1)}, ...) while((s32[]{:T(128)}, f32[3,256]{1,0:T(4,128)S(1)}, ...), condition=%wide.region_3.4_spmd.clone, body=%wide.region_0.3_spmd.clone.sunk | while | flops 205164320 | bytes 8636830 | solution.py:65
  657.0 1.2 constant_dynamic-slice_fusion.5
  659.1 0.6 convolution_add_fusion.2
  660.0 1.2 constant_dynamic-slice_fusion.5
  661.2 0.5 fusion.38
  662.0 0.6 convolution_add_fusion.2
  662.9 1.2 constant_dynamic-slice_fusion.5
  664.1 0.5 fusion.38
  664.9 0.6 convolution_add_fusion.2
  665.9 1.2 constant_dynamic-slice_fusion.5
  667.9 0.6 convolution_add_fusion.2
  668.8 1.2 constant_dynamic-slice_fusion.5
  670.8 0.6 convolution_add_fusion.2
  671.7 1.2 constant_dynamic-slice_fusion.5
  673.8 0.6 convolution_add_fusion.2
  674.7 1.2 constant_dynamic-slice_fusion.5
  676.7 0.6 convolution_add_fusion.2
  677.6 1.2 constant_dynamic-slice_fusion.5
  679.6 0.6 convolution_add_fusion.2
  680.5 1.2 constant_dynamic-slice_fusion.5
  682.5 0.6 convolution_add_fusion.2
  683.5 1.2 constant_dynamic-slice_fusion.5
  685.5 0.6 convolution_add_fusion.2
  686.4 1.2 constant_dynamic-slice_fusion.5
  688.4 0.6 convolution_add_fusion.2
  689.3 1.2 constant_dynamic-slice_fusion.5
  691.3 0.6 convolution_add_fusion.2
  692.3 1.2 constant_dynamic-slice_fusion.5
  694.3 0.6 convolution_add_fusion.2
  695.2 1.2 constant_dynamic-slice_fusion.5
  697.2 0.6 convolution_add_fusion.2
  698.1 1.2 constant_dynamic-slice_fusion.5
  700.1 0.6 convolution_add_fusion.2
  701.1 1.2 constant_dynamic-slice_fusion.5
  703.1 0.6 convolution_add_fusion.2
  704.0 35.9 %psum.7 = f32[256]{0:T(256)S(1)} all-reduce(f32[256]{0:T(256)S(1)} %get-tuple-element.268), channel_id=1, replica_groups=mesh['seq'=32,'head'=16] {'head'}, use_global_device_ids=true, to_apply=%region_7.8 | all-reduce | flops 256 | bytes 2048 | tf_op jit(solution)/shard_map/psum | solution.py:95
  740.1 0.8 copy.52
  (162 shorter events, 17.9 us)
Async XLA Ops:
  6.5 6.1 copy-start
  6.5 6.5 copy-start.1
  6.5 6.5 copy-start.3
  6.5 6.5 copy-start.2
  6.5 140.1 %all-gather.11.cloned.1.call-start = ((), (), s32[]{:S(2)}) async-start(), calls=%async_computation.3 | async-start | bytes 1622016 | tf_op jit(solution)/shard_map/all_gather | solution.py:67
  7.3 277.3 %all-gather.9.cloned.1.call-start = ((), (), s32[]{:S(2)}) async-start(), calls=%async_computation.2 | async-start | bytes 1622016 | tf_op jit(solution)/shard_map/all_gather | solution.py:68
  8.0 463.4 %all-gather.5.cloned.1.call-start = ((), (), s32[]{:S(2)}) async-start(), calls=%async_computation | async-start | bytes 6488064 | tf_op jit(solution)/shard_map/all_gather | solution.py:49
  9.8 647.0 %all-gather.7.cloned.1.call-start = ((), (), s32[]{:S(2)}) async-start(), calls=%async_computation.1 | async-start | bytes 6488064 | tf_op jit(solution)/shard_map/all_gather | solution.py:50
Sparse Core Ops, SparseCore 0:
  10.3 136.3 all-gather.10
  149.6 134.9 all-gather.8
  287.5 183.8 all-gather.4
  474.1 182.6 all-gather.6
where the time goes:
time: 748 us; the launch traced here: 747 us
  waiting for transfers between devices  639 us (85%)
  blocking collectives  35.9 us (5%)
  local copies, waits for them, and re-layouts  32.6 us (4%)
  matrix products  18.8 us (3%)
  between operations  13.3 us (2%)
    all_gather x1, waiting for transfers between devices, local(): value_piece = lax.all_gather(values, 'seq', axis=0, tiled=True)  185 us
    all_gather x1, waiting for transfers between devices, local(): key_piece = lax.all_gather(keys, 'seq', axis=0, tiled=True)  183 us
    all_gather x1, waiting for transfers between devices, local(): lax.all_gather(text_values, 'seq', axis=1, tiled=True)  136 us
    all_gather x1, waiting for transfers between devices, local(): lax.all_gather(text_keys, 'seq', axis=1, tiled=True)  134 us
    psum x1, blocking collectives, local(): square_total = lax.psum(squares, 'head')  35.9 us
    dynamic_slice x16, local copies, waits for them, and re-layouts, inner(): lax.dynamic_slice_in_dim(value_piece, offset, stride, 0)  18.8 us
  transfers between devices with their start and end apart: 4, of which 4 were waited for; matrix products, arithmetic and copies ran while one was open for 1% of the time, Pallas kernels for 0%

commit v1 on v0

v1 whole, which is shorter than its diff:
```python
import functools
import math

import jax
import jax.numpy as jnp
from jax import lax
from jax.experimental import pallas as pl
from jax.experimental.pallas import tpu as pltpu
from jax.sharding import PartitionSpec as P

HEADS = 48
HD = 128
BLK = 128
TOK = 256
NEG = 1e30
FACTOR = HD ** (-0.5) * math.log2(math.e)
MESH = pl.DeviceIdType.MESH
OFF = ((0, 3, 6), (9, 14, 11))
PARTS = ((0, 256), (256, 256), (512, 256), (768, 64), (832, 64))


def kernel(
    q_ref, k_ref, v_ref, tk_ref, tv_ref, meta_ref, gain_ref, out_ref,
    relay, relay_meta, qb, kb, tb, mb, bias, vt, tvt, scores, part, stat, got, got_stat, mine, home, sq,
    s1, r1, s2, r2, sx, rx, ss, rs, sq_s, sq_r, sm, rm, so, ro, sh, rh, sn, rn,
):
    s, hd = lax.axis_index("seq"), lax.axis_index("head")
    yhi, z = s // 16, s % 16
    ylo, x, core = hd // 8, (hd // 2) % 4, hd % 2
    col = hd // 2
    me_y = yhi * 2 + ylo
    me_m = hd % 8
    k = col + 8 * core
    zp = (k - z + 16) % 16
    partner = yhi * 16 + zp

    def at(y4, x4, c2):
        return ((y4 // 2) * 16 + z, (y4 % 2) * 8 + x4 * 2 + c2)

    def home_of(slot):
        first = (z - OFF[0][slot] + 16) % 16
        second = (z - OFF[1][slot] + 16) % 16
        even = first % 2 == 0
        return jnp.where(even, first, second + 1)

    def plane_of(slot):
        p = (2 * col + jnp.where(core == 0, OFF[0][slot], OFF[1][slot])) % 16
        kk = (z + p) % 16
        return p, (kk % 8) * 2 + kk // 8

    planes = [plane_of(i) for i in range(3)]
    homes = [home_of(i) for i in range(3)]

    barrier = pltpu.get_barrier_semaphore()

    def greet(device):
        pl.semaphore_signal(barrier, inc=1, device_id=device, device_id_type=MESH)

    for i in range(1, 16):
        greet((s, (hd + i) % 16))
    for d in (1, 2, 3):
        @pl.when((me_y + d) % 4 // 2 != yhi)
        def _():
            greet(at((me_y + d) % 4, x, core))
    count = 17
    far = zp != z

    @pl.when(far)
    def _():
        greet((partner, hd))

    count = count + jnp.where(far, 1, 0)
    for i in range(3):
        @pl.when(far)
        def _():
            greet((partner, homes[i]))

        apart = planes[i][0] != z

        @pl.when(apart)
        def _():
            greet((yhi * 16 + planes[i][0], planes[i][1]))

        count = count + jnp.where(far, 1, 0) + jnp.where(apart, 1, 0)
    pl.semaphore_wait(barrier, count)

    def remote(src, dst, send, recv, device):
        return pltpu.make_async_remote_copy(
            src_ref=src, dst_ref=dst, send_sem=send, recv_sem=recv, device_id=device, device_id_type=MESH
        )

    ends = []

    def push(src, dst, send, recv, device, here=None):
        copy = remote(src, dst, send, recv, device)
        if here is None:
            copy.start()
            ends.append((copy, None))
            return
        there = jnp.logical_not(here)

        @pl.when(there)
        def _():
            copy.start()

        @pl.when(here)
        def _():
            pltpu.make_async_copy(src, dst, recv).start()

        ends.append((copy, there))

    def landed(dst, recv):
        pltpu.make_async_copy(dst, dst, recv).wait()

    for slot in range(3):
        device = (s, planes[slot][1])
        here = planes[slot][1] == hd
        lanes = pl.ds(slot * HD, HD)
        for i, ref in ((1, k_ref), (2, v_ref), (3, tk_ref), (4, tv_ref), (0, q_ref)):
            low, rows = PARTS[i]
            push(ref.at[:, lanes], relay.at[slot, pl.ds(low, rows)], s1.at[slot, i], r1.at[slot, i], device, here)
        if slot == 0:
            push(meta_ref, relay_meta, s1.at[slot, 5], r1.at[slot, 5], device, here)

    def target(slot, i):
        return (
            qb.at[slot, me_y], kb.at[slot, 0, me_m], kb.at[slot, 1, me_m], tb.at[slot, 0, me_m], tb.at[slot, 1, me_m]
        )[i]

    for slot in range(3):
        for i in (1, 2, 3, 4, 0):
            low, rows = PARTS[i]
            src = relay.at[slot, pl.ds(low, rows)]
            landed(src, r1.at[slot, i])
            push(src, target(slot, i), s2.at[slot, i], r2.at[slot, i], (partner, hd), jnp.logical_not(far))
        if slot == 0:
            landed(relay_meta, r1.at[slot, 5])
            push(relay_meta, mb.at[me_y], s2.at[slot, 5], r2.at[slot, 5], (partner, hd), jnp.logical_not(far))

    def spread(slot):
        for i in (1, 2):
            landed(target(slot, i), r2.at[slot, i])
        chunk = kb.at[slot, :, me_m]
        for d in (2, 1, 3):
            push(chunk, chunk, sx.at[slot, d - 1, 0], rx.at[slot, d - 1, 0], at(me_y, (x + d) % 4, core))
        push(chunk, chunk, ss.at[slot, 0, 0], rs.at[slot, 0, 0], at(me_y, x, 1 - core))
        for i in (3, 4):
            landed(target(slot, i), r2.at[slot, i])
        text = tb.at[slot, :, me_m]
        for d in (2, 1, 3):
            push(text, text, sx.at[slot, d - 1, 1], rx.at[slot, d - 1, 1], at(me_y, (x + d) % 4, core))
        push(text, text, ss.at[slot, 0, 1], rs.at[slot, 0, 1], at(me_y, x, 1 - core))
        landed(target(slot, 0), r2.at[slot, 0])
        if slot == 0:
            landed(mb.at[me_y], r2.at[slot, 5])
        for d in (2, 1, 3):
            rows = qb.at[slot, me_y]
            push(rows, rows, sq_s.at[slot, d - 1], sq_r.at[slot, d - 1], at((me_y + d) % 4, x, core))
            if slot == 0:
                rows = mb.at[me_y]
                push(rows, rows, sm.at[d - 1], rm.at[d - 1], at((me_y + d) % 4, x, core))

    def pass_on(slot):
        for d in (1, 3, 2):
            m = (x - d + 4) % 4 * 2 + core
            for i, ref in ((0, kb), (1, tb)):
                chunk = ref.at[slot, :, m]
                landed(chunk, rx.at[slot, d - 1, i])
                push(chunk, chunk, ss.at[slot, d, i], rs.at[slot, d, i], at(me_y, x, 1 - core))

    def gathered(slot):
        for d in (1, 2, 3):
            rows = (me_y - d + 4) % 4
            landed(qb.at[slot, rows], sq_r.at[slot, d - 1])
            if slot == 0:
                landed(mb.at[rows], rm.at[d - 1])
        for d in range(4):
            m = (x - d + 4) % 4 * 2 + 1 - core
            for i, ref in ((0, kb), (1, tb)):
                landed(ref.at[slot, :, m], rs.at[slot, d, i])

    def masks():
        r = lax.broadcasted_iota(jnp.int32, (24, 128), 0)
        c = lax.broadcasted_iota(jnp.int32, (24, 128), 1)
        m = r >> 1
        km = ylo * 4 + (m >> 1) + 8 * (m & 1)
        block = 2 * (yhi * 16 + ((km - z + 16) & 15)) + (r & 1)
        pick = jnp.where(r < 16, block, 64 + r - 16) == c
        pick = pick.astype(jnp.float32).astype(jnp.bfloat16)
        rows = mb[...].reshape(32, 128).astype(jnp.bfloat16)
        by_block = lax.dot_general(pick, rows, (((1,), (1,)), ((), ())), preferred_element_type=jnp.float32)
        by_block = by_block.astype(jnp.bfloat16)
        row = lax.broadcasted_iota(jnp.int32, (32, TOK), 0)
        lane = lax.broadcasted_iota(jnp.int32, (32, TOK), 1)
        for j in range(4):
            spot = (row == 8 * j + (lane >> 7)).astype(jnp.float32).astype(jnp.bfloat16)
            ok = jnp.dot(by_block, spot, preferred_element_type=jnp.float32)
            bias[j] = (ok - 1.0) * NEG

    def compute(slot):
        for m in range(8):
            vt[:, m * TOK:(m + 1) * TOK] = kb[slot, 1, m].T
        for m in range(4):
            tvt[:, m * 128:(m + 1) * 128] = tb[slot, 1, 2 * m:2 * m + 2].reshape(128, HD).T

        def chunk(step, carry):
            j = (me_y + 1 + step) % 4
            rows = qb[slot, j]
            nt = (((1,), (1,)), ((), ()))
            t = lax.dot_general(tb[slot, 0].reshape(512, HD), rows, nt, preferred_element_type=jnp.float32)
            t = (t * FACTOR).reshape(8, 8, 8, TOK) + bias[j, 16:24].reshape(1, 8, 1, TOK)
            t = t.reshape(512, TOK)
            top = jnp.max(t, axis=0, keepdims=True)
            w = jnp.exp2(t - top)
            total = jnp.sum(w, axis=0, keepdims=True)
            acc = jnp.dot(tvt[...], w.astype(jnp.bfloat16), preferred_element_type=jnp.float32)
            part[slot, j, 1] = (acc / total).astype(jnp.bfloat16)
            stat[slot, j, 2:3] = top
            stat[slot, j, 3:4] = total
            top = None
            for m in range(8):
                t = lax.dot_general(kb[slot, 0, m], rows, nt, preferred_element_type=jnp.float32)
                t = (t * FACTOR).reshape(2, BLK, TOK) + bias[j, 2 * m:2 * m + 2].reshape(2, 1, TOK)
                t = t.reshape(TOK, TOK)
                scores[m] = t
                peak = jnp.max(t.reshape(32, 8, TOK), axis=0)
                top = peak if top is None else jnp.maximum(top, peak)
            top = jnp.max(top, axis=0, keepdims=True)
            total, acc = 0.0, 0.0
            for m in range(8):
                w = jnp.exp2(scores[m] - top)
                total = total + jnp.sum(w.reshape(32, 8, TOK), axis=0)
                acc = acc + jnp.dot(
                    vt[:, m * TOK:(m + 1) * TOK], w.astype(jnp.bfloat16), preferred_element_type=jnp.float32
                )
            total = jnp.sum(total, axis=0, keepdims=True)
            part[slot, j, 0] = (acc / total).astype(jnp.bfloat16)
            stat[slot, j, 0:1] = top
            stat[slot, j, 1:2] = total
            stat[slot, j, 4:8] = jnp.zeros((4, TOK), jnp.float32)

            @pl.when(step < 3)
            def _():
                remote(
                    part.at[slot, j], got.at[slot, me_y], so.at[slot, step, 0], ro.at[slot, step, 0], at(j, x, core)
                ).start()
                remote(
                    stat.at[slot, j], got_stat.at[slot, me_y], so.at[slot, step, 1], ro.at[slot, step, 1],
                    at(j, x, core),
                ).start()
            return carry

        lax.fori_loop(0, 4, chunk, 0)
        for d in (1, 2, 3):
            j = (me_y + d) % 4
            device = at(j, x, core)
            ends.append((remote(part.at[slot, j], got.at[slot, me_y], so.at[slot, d - 1, 0], ro.at[slot, d - 1, 0], device), None))
            ends.append((remote(stat.at[slot, j], got_stat.at[slot, me_y], so.at[slot, d - 1, 1], ro.at[slot, d - 1, 1], device), None))

    def combine(slot):
        parts, stats = [part.at[slot, me_y]], [stat[slot, me_y]]
        for d in (1, 2, 3):
            j = (me_y - d + 4) % 4
            landed(got.at[slot, j], ro.at[slot, d - 1, 0])
            landed(got_stat.at[slot, j], ro.at[slot, d - 1, 1])
            parts.append(got.at[slot, j])
            stats.append(got_stat[slot, j])
        total = 0.0
        for i in range(2):
            tops = [v[2 * i:2 * i + 1] for v in stats]
            top = functools.reduce(jnp.maximum, tops)
            share = [v[2 * i + 1:2 * i + 2] * jnp.exp2(t - top) for v, t in zip(stats, tops)]
            whole = 1.0 / functools.reduce(jnp.add, share)
            for v, w in zip(parts, share):
                total = total + v[i].astype(jnp.float32) * (w * whole)
        mine[slot] = total.astype(jnp.bfloat16)
        here = jnp.logical_and(jnp.logical_not(far), homes[slot] == hd)
        push(mine.at[slot], home.at[slot], sh.at[slot], rh.at[slot], (partner, homes[slot]), here)

    spread(0)
    pass_on(0)
    gathered(0)
    masks()
    compute(0)
    spread(1)
    combine(0)
    pass_on(1)
    gathered(1)
    compute(1)
    spread(2)
    combine(1)
    pass_on(2)
    gathered(2)
    compute(2)
    combine(2)

    squares = 0.0
    for slot in range(3):
        landed(home.at[slot], rh.at[slot])
        v = home[slot].astype(jnp.float32)
        squares = squares + jnp.sum(v * v, axis=0, keepdims=True)
    sq[hd] = jnp.concatenate([squares[:, :128], squares[:, 128:], jnp.zeros((6, 128), jnp.float32)], axis=0)
    for d in range(1, 16):
        push(sq.at[hd], sq.at[hd], sn.at[d - 1], rn.at[d - 1], (s, (hd + d) % 16))
    for d in range(1, 16):
        landed(sq.at[(hd - d + 16) % 16], rn.at[d - 1])
    whole = jnp.sum(sq[...], axis=0)
    inv = lax.rsqrt(whole / (HEADS * HD) + 1e-06)
    inv = jnp.concatenate([inv[0:1], inv[1:2]], axis=1)
    for slot in range(3):
        v = (home[slot].astype(jnp.float32) * inv).T
        lanes = slice(slot * HD, (slot + 1) * HD)
        out_ref[:, lanes] = (v * gain_ref[:, lanes]).astype(jnp.bfloat16)
    for copy, there in ends:
        if there is None:
            copy.wait_send()
        else:
            pl.when(there)(copy.wait_send)


def local(queries, keys, values, block_mask, region_of_block, text_keys, text_values, gain):
    first = lax.axis_index("seq") * 2
    columns = jnp.arange(64, dtype=jnp.int32)
    owned = first + jnp.arange(2, dtype=jnp.int32)
    allowed = (block_mask > 0) | (columns[None, :] == owned[:, None])
    region = region_of_block[:, None] == jnp.arange(64, dtype=jnp.int32)[None, :]
    meta = jnp.concatenate([allowed, region], axis=1).astype(jnp.float32)
    meta = jnp.pad(meta, ((0, 6), (0, 0)))
    bf, f32 = jnp.bfloat16, jnp.float32
    dma = pltpu.SemaphoreType.DMA
    vmem = pl.BlockSpec(memory_space=pltpu.VMEM)
    hbm = pl.BlockSpec(memory_space=pl.ANY)
    return pl.pallas_call(
        kernel,
        out_shape=jax.ShapeDtypeStruct((TOK, 3 * HD), bf),
        in_specs=[hbm, hbm, hbm, hbm, hbm, vmem, vmem],
        out_specs=vmem,
        scratch_shapes=[
            pltpu.VMEM((3, 896, HD), bf),
            pltpu.VMEM((8, 128), f32),
            pltpu.VMEM((3, 4, TOK, HD), bf),
            pltpu.VMEM((3, 2, 8, TOK, HD), bf),
            pltpu.VMEM((3, 2, 8, 64, HD), bf),
            pltpu.VMEM((4, 8, 128), f32),
            pltpu.VMEM((4, 24, TOK), f32),
            pltpu.VMEM((HD, 8 * TOK), bf),
            pltpu.VMEM((HD, 512), bf),
            pltpu.VMEM((8, TOK, TOK), f32),
            pltpu.VMEM((3, 4, 2, HD, TOK), bf),
            pltpu.VMEM((3, 4, 8, TOK), f32),
            pltpu.VMEM((3, 4, 2, HD, TOK), bf),
            pltpu.VMEM((3, 4, 8, TOK), f32),
            pltpu.VMEM((3, HD, TOK), bf),
            pltpu.VMEM((3, HD, TOK), bf),
            pltpu.VMEM((16, 8, 128), f32),
            dma((3, 6)), dma((3, 6)),
            dma((3, 6)), dma((3, 6)),
            dma((3, 3, 2)), dma((3, 3, 2)),
            dma((3, 4, 2)), dma((3, 4, 2)),
            dma((3, 3)), dma((3, 3)),
            dma((3,)), dma((3,)),
            dma((3, 3, 2)), dma((3, 3, 2)),
            dma((3,)), dma((3,)),
            dma((15,)), dma((15,)),
        ],
        compiler_params=pltpu.CompilerParams(
            collective_id=0, has_side_effects=True, vmem_limit_bytes=40 * 2**20
        ),
        name="attend",
    )(
        queries, keys, values, text_keys.reshape(64, 3 * HD), text_values.reshape(64, 3 * HD), meta,
        gain.astype(f32)[None, :],
    )


def solution(mesh):
    in_specs = (
        P("seq", "head"),
        P("seq", "head"),
        P("seq", "head"),
        P("seq", None),
        P("seq"),
        P(None, "seq", "head"),
        P(None, "seq", "head"),
        P("head"),
    )
    out_specs = P("seq", "head")
    return jax.shard_map(local, mesh=mesh, in_specs=in_specs, out_specs=out_specs, check_vma=False)
```

time: 748 us -> 128 us (0.17)
  waiting for transfers between devices: 639 us -> 0 us
  Pallas kernels: 0 us -> 120 us
  blocking collectives: 35.9 us -> 0 us
  local copies, waits for them, and re-layouts: 32.6 us -> 6.33 us
  matrix products: 18.8 us -> 0 us
  between operations: 13.3 us -> 0.03 us
    all_gather x4 -> x0, waiting for transfers between devices: 638 us -> none  [the longest x1 185 us: local(): value_piece = lax.all_gather(values, 'seq', axis=0, tiled=True)]
    pallas_call x0 -> x1, Pallas kernels: none -> 120 us  [local(): pl.pallas_call(kernel, out_shape=jax.ShapeDtypeStruct((TOK, 3 * HD), bf),...]
    psum x1 -> x0, blocking collectives: 35.9 us -> none  [local(): square_total = lax.psum(squares, 'head')]
    dynamic_slice x32 -> x0, local copies, waits for them, and re-layouts: 20 us -> none  [the longest x16 18.8 us: inner(): lax.dynamic_slice_in_dim(value_piece, offset, stride, 0)]
    dot_general x34 -> x0, matrix products: 18.8 us -> none  [the longest x16 10.4 us: absorb(): jnp.einsum('hqk,khd->hqd', weights.astype(jnp.bfloat16), value_block, pre...]
  transfers between devices with their start and end apart: 4 -> 0, of which waited for: 4 -> 0; matrix products, arithmetic and copies ran while one was open for 1% -> 0% of each run, Pallas kernels for 0% -> 0%
where the time goes in v1:
time: 128 us; the launch traced here: 127 us
  Pallas kernels  120 us (94%)
  local copies, waits for them, and re-layouts  6.33 us (5%)
    pallas_call x1, Pallas kernels, local(): pl.pallas_call(kernel, out_shape=jax.ShapeDtypeStruct((TOK, 3 * HD), bf),...  120 us
    unnamed x17, local copies, waits for them, and re-layouts  6.33 us

profile of v1, /device:TPU:1, one launch (start us, length us, event | category | flops | bytes accessed | tf_op | source)
XLA Modules:
  0.0 126.9 jit_solution(10916198823809310067)
XLA Ops:
  0.0 0.0 copy-start.5
  0.0 0.0 copy-start.7
  0.0 0.7 copy-done.5
  0.7 0.0 copy-done.7
  0.7 0.1 compare_or_fusion
  0.8 0.0 copy-start.6
  0.8 0.1 pad_add_fusion
  0.8 0.6 copy-done.6
  1.5 0.0 copy-start
  1.5 0.9 copy-done
  2.4 0.0 copy-start.1
  2.4 0.9 copy-done.1
  3.3 0.0 copy-start.2
  3.3 0.9 copy-done.2
  4.2 0.0 copy-start.3
  4.2 0.8 copy-done.3
  5.0 0.0 copy-start.4
  5.0 0.8 copy-done.4
  5.8 120.4 %attend.1 = bf16[256,384]{1,0:T(8,128)(2,1)S(1)} custom-call(bf16[256,384]{1,0:T(8,128)(2,1)S(1)} %copy-done, bf16[256,384]{1,0:T(8,128)(2,1)S(1)} %copy-done.1, bf16[256,384]{1,0:T(8,128)(2,1)S(1)} %copy-done.2, bf16[64,384]{1,0:T(8,128)(2,1)S(1)} %bitcast.2, bf16[64,384]{1,0:T(8,128)(2,1)S(1)} %bitcast.3, f32[8,128]{1,0:T(8,128)S(1)} %pad_convert_fusion.meta_ref, ...), custom_call_target="tpu_custom_call" | custom-call | tf_op jit(solution)/shard_map/attend/pallas_call | solution.py:333
  126.2 0.7 copy.10
  (3 shorter events, 0.0 us)
Async XLA Ops:
  0.0 0.7 copy-start.5
  0.0 0.7 copy-start.7
  0.8 0.7 copy-start.6
  1.5 0.9 copy-start
  2.4 0.9 copy-start.1
  3.3 0.9 copy-start.2
  4.2 0.8 copy-start.3
  5.0 0.8 copy-start.4

commit v2 on v1

v2 whole, which is shorter than its diff:
```python
import functools
import math

import jax
import jax.numpy as jnp
from jax import lax
from jax.experimental import pallas as pl
from jax.experimental.pallas import tpu as pltpu
from jax.sharding import PartitionSpec as P

HEADS = 48
HD = 128
BLK = 128
TOK = 256
NEG = 1e30
FACTOR = HD ** (-0.5) * math.log2(math.e)
MESH = pl.DeviceIdType.MESH
OFF = ((0, 3, 6), (9, 14, 11))
PARTS = ((0, 256), (256, 256), (512, 256), (768, 64), (832, 64))


def kernel(
    q_ref, k_ref, v_ref, tk_ref, tv_ref, mask_ref, region_ref, gain_ref, out_ref,
    meta, relay, relay_meta, qb, kb, tb, mb, bias, vt, tvt, scores, weights, sums, turned, part, stat, got, got_stat, mine, home, sq,
    s1, r1, s2, r2, sx, rx, ss, rs, sq_s, sq_r, sm, rm, so, ro, sh, rh, sn, rn,
):
    s, hd = lax.axis_index("seq"), lax.axis_index("head")
    yhi, z = s // 16, s % 16
    ylo, x, core = hd // 8, (hd // 2) % 4, hd % 2
    col = hd // 2
    me_y = yhi * 2 + ylo
    me_m = hd % 8
    k = jnp.where(core == 0, col, 8 + (col ^ 1))
    zp = (k - z + 16) % 16
    partner = yhi * 16 + zp

    def at(y4, x4, c2):
        return ((y4 // 2) * 16 + z, (y4 % 2) * 8 + x4 * 2 + c2)

    def home_of(slot):
        first = (z - OFF[0][slot] + 16) % 16
        second = (z - OFF[1][slot] + 16) % 16
        even = first % 2 == 0
        return jnp.where(even, first, second + 1)

    def plane_of(slot):
        p = (2 * col + jnp.where(core == 0, OFF[0][slot], OFF[1][slot])) % 16
        kk = (z + p) % 16
        return p, jnp.where(kk < 8, kk * 2, ((kk - 8) ^ 1) * 2 + 1)

    planes = [plane_of(i) for i in range(3)]
    homes = [home_of(i) for i in range(3)]

    meta[...] = jnp.zeros((8, 128), jnp.float32)
    lane = lax.broadcasted_iota(jnp.int32, (2, 64), 1)
    row = lax.broadcasted_iota(jnp.int32, (2, 64), 0)
    meta[0:2, 0:64] = jnp.logical_or(mask_ref[...] > 0, lane == 2 * s + row).astype(jnp.float32)
    meta[0:2, 64:128] = (lane == jnp.where(row == 0, region_ref[0], region_ref[1])).astype(jnp.float32)

    barrier = pltpu.get_barrier_semaphore()

    def greet(device):
        pl.semaphore_signal(barrier, inc=1, device_id=device, device_id_type=MESH)

    for i in range(1, 16):
        greet((s, (hd + i) % 16))
    for d in (1, 2, 3):
        @pl.when((me_y + d) % 4 // 2 != yhi)
        def _():
            greet(at((me_y + d) % 4, x, core))
    count = 17
    far = zp != z

    @pl.when(far)
    def _():
        greet((partner, hd))

    count = count + jnp.where(far, 1, 0)
    for i in range(3):
        @pl.when(far)
        def _():
            greet((partner, homes[i]))

        apart = planes[i][0] != z

        @pl.when(apart)
        def _():
            greet((yhi * 16 + planes[i][0], planes[i][1]))

        count = count + jnp.where(far, 1, 0) + jnp.where(apart, 1, 0)
    pl.semaphore_wait(barrier, count)

    def remote(src, dst, send, recv, device):
        return pltpu.make_async_remote_copy(
            src_ref=src, dst_ref=dst, send_sem=send, recv_sem=recv, device_id=device, device_id_type=MESH
        )

    ends = []

    def push(src, dst, send, recv, device, here=None):
        copy = remote(src, dst, send, recv, device)
        if here is None:
            copy.start()
            ends.append((copy, None))
            return
        there = jnp.logical_not(here)

        @pl.when(there)
        def _():
            copy.start()

        @pl.when(here)
        def _():
            pltpu.make_async_copy(src, dst, recv).start()

        ends.append((copy, there))

    def landed(dst, recv):
        pltpu.make_async_copy(dst, dst, recv).wait()

    def give(slot):
        device = (s, planes[slot][1])
        here = planes[slot][1] == hd
        lanes = pl.ds(slot * HD, HD)
        for i, ref in ((0, q_ref), (3, tk_ref), (4, tv_ref), (1, k_ref), (2, v_ref)):
            low, rows = PARTS[i]
            push(ref.at[:, lanes], relay.at[slot, pl.ds(low, rows)], s1.at[slot, i], r1.at[slot, i], device, here)
        if slot == 0:
            push(meta, relay_meta, s1.at[slot, 5], r1.at[slot, 5], device, here)

    def target(slot, i):
        return (
            qb.at[slot, me_y], kb.at[slot, 0, me_m], kb.at[slot, 1, me_m], tb.at[slot, 0, me_m], tb.at[slot, 1, me_m]
        )[i]

    def forward(slot, i):
        low, rows = PARTS[i]
        src = relay.at[slot, pl.ds(low, rows)]
        landed(src, r1.at[slot, i])
        push(src, target(slot, i), s2.at[slot, i], r2.at[slot, i], (partner, hd), jnp.logical_not(far))
        if slot == 0 and i == 0:
            landed(relay_meta, r1.at[slot, 5])
            push(relay_meta, mb.at[me_y], s2.at[slot, 5], r2.at[slot, 5], (partner, hd), jnp.logical_not(far))

    def piece(slot, i, m):
        return tb.at[slot, :, m] if i == 2 else kb.at[slot, i, m]

    def spread(slot, i):
        lands = ((1,), (2,), (3, 4))[i]
        for part_id in lands:
            landed(target(slot, part_id), r2.at[slot, part_id])
        chunk = piece(slot, i, me_m)
        for d in (2, 1, 3):
            push(chunk, chunk, sx.at[slot, d - 1, i], rx.at[slot, d - 1, i], at(me_y, (x + d) % 4, core))
        push(chunk, chunk, ss.at[slot, 0, i], rs.at[slot, 0, i], at(me_y, x, 1 - core))
        if slot < 2:
            for part_id in lands:
                forward(slot + 1, part_id)

    def spread_queries(slot):
        landed(target(slot, 0), r2.at[slot, 0])
        if slot == 0:
            landed(mb.at[me_y], r2.at[slot, 5])
        for d in (2, 1, 3):
            rows = qb.at[slot, me_y]
            push(rows, rows, sq_s.at[slot, d - 1], sq_r.at[slot, d - 1], at((me_y + d) % 4, x, core))
            if slot == 0:
                rows = mb.at[me_y]
                push(rows, rows, sm.at[d - 1], rm.at[d - 1], at((me_y + d) % 4, x, core))
        if slot < 2:
            forward(slot + 1, 0)

    def pass_on(slot, i):
        for d in (1, 3, 2):
            chunk = piece(slot, i, (x - d + 4) % 4 * 2 + core)
            landed(chunk, rx.at[slot, d - 1, i])
            push(chunk, chunk, ss.at[slot, d, i], rs.at[slot, d, i], at(me_y, x, 1 - core))

    def gathered(slot, i):
        for d in range(4):
            landed(piece(slot, i, (x - d + 4) % 4 * 2 + 1 - core), rs.at[slot, d, i])

    def gathered_queries(slot):
        for d in (1, 2, 3):
            rows = (me_y - d + 4) % 4
            landed(qb.at[slot, rows], sq_r.at[slot, d - 1])
            if slot == 0:
                landed(mb.at[rows], rm.at[d - 1])

    def masks():
        r = lax.broadcasted_iota(jnp.int32, (24, 128), 0)
        c = lax.broadcasted_iota(jnp.int32, (24, 128), 1)
        m = r >> 1
        column = ylo * 4 + (m >> 1)
        km = jnp.where((m & 1) == 0, column, 8 + (column ^ 1))
        block = 2 * (yhi * 16 + ((km - z + 16) & 15)) + (r & 1)
        pick = jnp.where(r < 16, block, 64 + r - 16) == c
        pick = pick.astype(jnp.float32).astype(jnp.bfloat16)
        rows = mb[...].reshape(32, 128).astype(jnp.bfloat16)
        by_block = lax.dot_general(pick, rows, (((1,), (1,)), ((), ())), preferred_element_type=jnp.float32)
        by_block = by_block.astype(jnp.bfloat16)
        row = lax.broadcasted_iota(jnp.int32, (32, TOK), 0)
        lane = lax.broadcasted_iota(jnp.int32, (32, TOK), 1)
        for j in range(4):
            spot = (row == 8 * j + (lane >> 7)).astype(jnp.float32).astype(jnp.bfloat16)
            ok = jnp.dot(by_block, spot, preferred_element_type=jnp.float32)
            bias[j] = (ok - 1.0) * NEG

    nt = (((1,), (1,)), ((), ()))

    def ship(slot, step, j, src, dst, i):
        @pl.when(step < 3)
        def _():
            remote(src, dst, so.at[slot, step, i], ro.at[slot, step, i], at(j, x, core)).start()

    def text(slot):
        for m in range(4):
            tvt[:, m * 128:(m + 1) * 128] = tb[slot, 1, 2 * m:2 * m + 2].reshape(128, HD).T

        def chunk(step, carry):
            j = (me_y + 1 + step) % 4
            t = lax.dot_general(tb[slot, 0].reshape(512, HD), qb[slot, j], nt, preferred_element_type=jnp.float32)
            t = (t * FACTOR).reshape(8, 8, 8, TOK) + bias[j, 16:24].reshape(1, 8, 1, TOK)
            t = t.reshape(512, TOK)
            top = jnp.max(t, axis=0, keepdims=True)
            w = jnp.exp2(t - top)
            total = jnp.sum(w, axis=0, keepdims=True)
            acc = jnp.dot(tvt[...], w.astype(jnp.bfloat16), preferred_element_type=jnp.float32)
            part[slot, j, 1] = (acc / total).astype(jnp.bfloat16)
            stat[slot, j, 2:3] = top
            stat[slot, j, 3:4] = total
            stat[slot, j, 4:8] = jnp.zeros((4, TOK), jnp.float32)
            ship(slot, step, j, part.at[slot, j, 1], got.at[slot, me_y, 1], 2)
            return carry

        lax.fori_loop(0, 4, chunk, 0)

    def score(slot):
        def chunk(step, carry):
            j = (me_y + 1 + step) % 4
            rows = qb[slot, j]
            top = None
            for m in range(8):
                t = lax.dot_general(kb[slot, 0, m], rows, nt, preferred_element_type=jnp.float32)
                t = (t * FACTOR).reshape(2, BLK, TOK) + bias[j, 2 * m:2 * m + 2].reshape(2, 1, TOK)
                t = t.reshape(TOK, TOK)
                scores[m] = t
                peak = jnp.max(t.reshape(32, 8, TOK), axis=0)
                top = peak if top is None else jnp.maximum(top, peak)
            top = jnp.max(top, axis=0, keepdims=True)
            total = 0.0
            for m in range(8):
                w = jnp.exp2(scores[m] - top)
                total = total + jnp.sum(w.reshape(32, 8, TOK), axis=0)
                weights[j, m * TOK:(m + 1) * TOK] = w.astype(jnp.bfloat16)
            total = jnp.sum(total, axis=0, keepdims=True)
            stat[slot, j, 0:1] = top
            stat[slot, j, 1:2] = total
            ship(slot, step, j, stat.at[slot, j], got_stat.at[slot, me_y], 1)
            return carry

        lax.fori_loop(0, 4, chunk, 0)

    def weigh(slot):
        for m in range(8):
            vt[:, m * TOK:(m + 1) * TOK] = kb[slot, 1, m].T

        def chunk(step, carry):
            j = (me_y + 1 + step) % 4
            acc = jnp.dot(vt[...], weights[j], preferred_element_type=jnp.float32)
            part[slot, j, 0] = (acc / stat[slot, j, 1:2]).astype(jnp.bfloat16)
            ship(slot, step, j, part.at[slot, j, 0], got.at[slot, me_y, 0], 0)
            return carry

        lax.fori_loop(0, 4, chunk, 0)
        for d in (1, 2, 3):
            j = (me_y + d) % 4
            for i, src, dst in (
                (0, part.at[slot, j, 0], got.at[slot, me_y, 0]),
                (1, stat.at[slot, j], got_stat.at[slot, me_y]),
                (2, part.at[slot, j, 1], got.at[slot, me_y, 1]),
            ):
                ends.append((remote(src, dst, so.at[slot, d - 1, i], ro.at[slot, d - 1, i], at(j, x, core)), None))

    def combine(slot):
        parts, stats = [part.at[slot, me_y]], [stat[slot, me_y]]
        for d in (1, 2, 3):
            j = (me_y - d + 4) % 4
            landed(got.at[slot, j, 1], ro.at[slot, d - 1, 2])
            landed(got_stat.at[slot, j], ro.at[slot, d - 1, 1])
            landed(got.at[slot, j, 0], ro.at[slot, d - 1, 0])
            parts.append(got.at[slot, j])
            stats.append(got_stat[slot, j])
        total = 0.0
        for i in range(2):
            tops = [v[2 * i:2 * i + 1] for v in stats]
            top = functools.reduce(jnp.maximum, tops)
            share = [v[2 * i + 1:2 * i + 2] * jnp.exp2(t - top) for v, t in zip(stats, tops)]
            whole = 1.0 / functools.reduce(jnp.add, share)
            for v, w in zip(parts, share):
                total = total + v[i].astype(jnp.float32) * (w * whole)
        mine[slot] = total.astype(jnp.bfloat16)
        here = jnp.logical_and(jnp.logical_not(far), homes[slot] == hd)
        push(mine.at[slot], home.at[slot], sh.at[slot], rh.at[slot], (partner, homes[slot]), here)

    def take(slot):
        landed(home.at[slot], rh.at[slot])
        v = home[slot].astype(jnp.float32)
        found = jnp.sum(v * v, axis=0, keepdims=True)
        sums[...] = found if slot == 0 else sums[...] + found

    def turn(slot):
        lanes = slice(slot * HD, (slot + 1) * HD)
        turned[:, lanes] = home[slot].astype(jnp.float32).T * gain_ref[:, lanes].astype(jnp.float32)

    give(0)
    for i in (0, 3, 4, 1, 2):
        forward(0, i)
    give(1)
    for slot in range(3):
        spread_queries(slot)
        spread(slot, 2)
        if slot == 0:
            give(2)
        else:
            gathered(slot - 1, 1)
            weigh(slot - 1)
        pass_on(slot, 2)
        spread(slot, 0)
        gathered_queries(slot)
        if slot == 0:
            masks()
        gathered(slot, 2)
        text(slot)
        pass_on(slot, 0)
        spread(slot, 1)
        if slot > 0:
            combine(slot - 1)
        gathered(slot, 0)
        score(slot)
        pass_on(slot, 1)
    gathered(2, 1)
    weigh(2)
    take(0)
    turn(0)
    take(1)
    turn(1)
    combine(2)
    take(2)

    squares = sums[...]
    sq[hd] = jnp.concatenate([squares[:, :128], squares[:, 128:], jnp.zeros((6, 128), jnp.float32)], axis=0)
    for d in range(1, 16):
        push(sq.at[hd], sq.at[hd], sn.at[d - 1], rn.at[d - 1], (s, (hd + d) % 16))
    turn(2)
    for d in range(1, 16):
        landed(sq.at[(hd - d + 16) % 16], rn.at[d - 1])
    whole = jnp.sum(sq[...], axis=0)
    inv = lax.rsqrt(whole / (HEADS * HD) + 1e-06)
    inv = jnp.broadcast_to(jnp.concatenate([inv[0:1], inv[1:2]], axis=1), (HD, TOK)).T
    for slot in range(3):
        lanes = slice(slot * HD, (slot + 1) * HD)
        out_ref[:, lanes] = (turned[:, lanes] * inv).astype(jnp.bfloat16)
    for copy, there in ends:
        if there is None:
            copy.wait_send()
        else:
            pl.when(there)(copy.wait_send)


def local(queries, keys, values, block_mask, region_of_block, text_keys, text_values, gain):
    bf, f32 = jnp.bfloat16, jnp.float32
    dma = pltpu.SemaphoreType.DMA
    vmem = pl.BlockSpec(memory_space=pltpu.VMEM)
    hbm = pl.BlockSpec(memory_space=pltpu.HBM)
    return pl.pallas_call(
        kernel,
        out_shape=jax.ShapeDtypeStruct((TOK, 3 * HD), bf),
        in_specs=[hbm, hbm, hbm, hbm, hbm, vmem, pl.BlockSpec(memory_space=pltpu.SMEM), vmem],
        out_specs=vmem,
        scratch_shapes=[
            pltpu.VMEM((8, 128), f32),
            pltpu.VMEM((3, 896, HD), bf),
            pltpu.VMEM((8, 128), f32),
            pltpu.VMEM((3, 4, TOK, HD), bf),
            pltpu.VMEM((3, 2, 8, TOK, HD), bf),
            pltpu.VMEM((3, 2, 8, 64, HD), bf),
            pltpu.VMEM((4, 8, 128), f32),
            pltpu.VMEM((4, 24, TOK), f32),
            pltpu.VMEM((HD, 8 * TOK), bf),
            pltpu.VMEM((HD, 512), bf),
            pltpu.VMEM((8, TOK, TOK), f32),
            pltpu.VMEM((4, 8 * TOK, TOK), bf),
            pltpu.VMEM((1, TOK), f32),
            pltpu.VMEM((TOK, 3 * HD), f32),
            pltpu.VMEM((3, 4, 2, HD, TOK), bf),
            pltpu.VMEM((3, 4, 8, TOK), f32),
            pltpu.VMEM((3, 4, 2, HD, TOK), bf),
            pltpu.VMEM((3, 4, 8, TOK), f32),
            pltpu.VMEM((3, HD, TOK), bf),
            pltpu.VMEM((3, HD, TOK), bf),
            pltpu.VMEM((16, 8, 128), f32),
            dma((3, 6)), dma((3, 6)),
            dma((3, 6)), dma((3, 6)),
            dma((3, 3, 3)), dma((3, 3, 3)),
            dma((3, 4, 3)), dma((3, 4, 3)),
            dma((3, 3)), dma((3, 3)),
            dma((3,)), dma((3,)),
            dma((3, 3, 3)), dma((3, 3, 3)),
            dma((3,)), dma((3,)),
            dma((15,)), dma((15,)),
        ],
        compiler_params=pltpu.CompilerParams(
            collective_id=0, has_side_effects=True, vmem_limit_bytes=60 * 2**20
        ),
        name="attend",
    )(
        queries, keys, values, text_keys.reshape(64, 3 * HD), text_values.reshape(64, 3 * HD),
        block_mask, region_of_block, gain[None, :],
    )


def solution(mesh):
    in_specs = (
        P("seq", "head"),
        P("seq", "head"),
        P("seq", "head"),
        P("seq", None),
        P("seq"),
        P(None, "seq", "head"),
        P(None, "seq", "head"),
        P("head"),
    )
    out_specs = P("seq", "head")
    return jax.shard_map(local, mesh=mesh, in_specs=in_specs, out_specs=out_specs, check_vma=False)
```

time: 128 us -> 109 us (0.85)
  Pallas kernels: 120 us -> 106 us
  local copies, waits for them, and re-layouts: 6.33 us -> 2.87 us
    pallas_call x1, Pallas kernels: 120 us -> 106 us  [local(): pl.pallas_call(kernel, out_shape=jax.ShapeDtypeStruct((TOK, 3 * HD), bf),...]
    unnamed x17 -> x3, local copies, waits for them, and re-layouts: 6.33 us -> 2.3 us
where the time goes in v2:
time: 109 us
  Pallas kernels  106 us (97%)
  local copies, waits for them, and re-layouts  2.87 us (3%)
    pallas_call x1, Pallas kernels, local(): pl.pallas_call(kernel, out_shape=jax.ShapeDtypeStruct((TOK, 3 * HD), bf),...  106 us
    unnamed x3, local copies, waits for them, and re-layouts  2.3 us

profile of v2, /device:TPU:1, one launch (start us, length us, event | category | flops | bytes accessed | tf_op | source)
XLA Modules:
  0.0 108.8 jit_solution(7642465553435938993)
XLA Ops:
  0.0 0.0 copy-start
  0.0 0.7 copy-done
  0.7 0.6 broadcast_in_dim.3.gain_ref
  1.2 105.9 %attend.1 = bf16[256,384]{1,0:T(8,128)(2,1)} custom-call(bf16[256,384]{1,0:T(8,128)(2,1)} %q_ref.1, bf16[256,384]{1,0:T(8,128)(2,1)} %k_ref.1, bf16[256,384]{1,0:T(8,128)(2,1)} %v_ref.1, bf16[64,384]{1,0:T(8,128)(2,1)} %bitcast.2, bf16[64,384]{1,0:T(8,128)(2,1)} %bitcast.3, s32[2,64]{1,0:T(2,128)} %mask_ref.1, s32[2]{0:T(128)} %region_ref.1, ...), custom_call_target="tpu_custom_call" | custom-call | tf_op jit(solution)/shard_map/attend/pallas_call | solution.py:376
  107.1 1.6 %copy.10 = bf16[256,384]{1,0:T(8,128)(2,1)} copy(bf16[256,384]{1,0:T(8,128)(2,1)} %attend.1) | data formatting | bytes 393216
Async XLA Ops:
  0.0 0.7 copy-start

commit v3 on v2

--- a/solution.py
+++ b/solution.py
@@ -15,6 +15,8 @@
 NEG = 1e30
 FACTOR = HD ** (-0.5) * math.log2(math.e)
 MESH = pl.DeviceIdType.MESH
+GROUPS = ((0, 3, 4), (1,), (2,))
+WINDOW = 2
 OFF = ((0, 3, 6), (9, 14, 11))
 PARTS = ((0, 256), (256, 256), (512, 256), (768, 64), (832, 64))
 
@@ -153,9 +155,10 @@
         for d in (2, 1, 3):
             push(chunk, chunk, sx.at[slot, d - 1, i], rx.at[slot, d - 1, i], at(me_y, (x + d) % 4, core))
         push(chunk, chunk, ss.at[slot, 0, i], rs.at[slot, 0, i], at(me_y, x, 1 - core))
-        if slot < 2:
-            for part_id in lands:
-                forward(slot + 1, part_id)
+        later = 3 * slot + (1, 2, 0)[i] + WINDOW
+        if later < 9:
+            for part_id in GROUPS[later % 3]:
+                forward(later // 3, part_id)
 
     def spread_queries(slot):
         landed(target(slot, 0), r2.at[slot, 0])
@@ -167,8 +170,6 @@
             if slot == 0:
                 rows = mb.at[me_y]
                 push(rows, rows, sm.at[d - 1], rm.at[d - 1], at((me_y + d) % 4, x, core))
-        if slot < 2:
-            forward(slot + 1, 0)
 
     def pass_on(slot, i):
         for d in (1, 3, 2):
@@ -314,8 +315,9 @@
         turned[:, lanes] = home[slot].astype(jnp.float32).T * gain_ref[:, lanes].astype(jnp.float32)
 
     give(0)
-    for i in (0, 3, 4, 1, 2):
-        forward(0, i)
+    for first in range(WINDOW):
+        for i in GROUPS[first]:
+            forward(0, i)
     give(1)
     for slot in range(3):
         spread_queries(slot)
@@ -334,11 +336,11 @@
         text(slot)
         pass_on(slot, 0)
         spread(slot, 1)
-        if slot > 0:
-            combine(slot - 1)
         gathered(slot, 0)
         score(slot)
         pass_on(slot, 1)
+        if slot > 0:
+            combine(slot - 1)
     gathered(2, 1)
     weigh(2)
     take(0)

time: 109 us -> 108 us (level)
    pallas_call x1, Pallas kernels: 106 us -> 105 us  [local(): pl.pallas_call(kernel, out_shape=jax.ShapeDtypeStruct((TOK, 3 * HD), bf),...]
where the time goes in v3:
time: 108 us; the launch traced here: 107 us
  Pallas kernels  105 us (97%)
  local copies, waits for them, and re-layouts  2.87 us (3%)
    pallas_call x1, Pallas kernels, local(): pl.pallas_call(kernel, out_shape=jax.ShapeDtypeStruct((TOK, 3 * HD), bf),...  105 us
    unnamed x3, local copies, waits for them, and re-layouts  2.3 us

profile of v3, /device:TPU:1, one launch (start us, length us, event | category | flops | bytes accessed | tf_op | source)
XLA Modules:
  0.0 107.4 jit_solution(2229996797113897373)
XLA Ops:
  0.0 0.0 copy-start
  0.0 0.7 copy-done
  0.7 0.6 broadcast_in_dim.3.gain_ref
  1.2 104.6 %attend.1 = bf16[256,384]{1,0:T(8,128)(2,1)} custom-call(bf16[256,384]{1,0:T(8,128)(2,1)} %q_ref.1, bf16[256,384]{1,0:T(8,128)(2,1)} %k_ref.1, bf16[256,384]{1,0:T(8,128)(2,1)} %v_ref.1, bf16[64,384]{1,0:T(8,128)(2,1)} %bitcast.2, bf16[64,384]{1,0:T(8,128)(2,1)} %bitcast.3, s32[2,64]{1,0:T(2,128)} %mask_ref.1, s32[2]{0:T(128)} %region_ref.1, ...), custom_call_target="tpu_custom_call" | custom-call | tf_op jit(solution)/shard_map/attend/pallas_call | solution.py:378
  105.8 1.6 %copy.10 = bf16[256,384]{1,0:T(8,128)(2,1)} copy(bf16[256,384]{1,0:T(8,128)(2,1)} %attend.1) | data formatting | bytes 393216
Async XLA Ops:
  0.0 0.7 copy-start
